TPU v7x, 256 devices: a whole 4x4x8 slice. The times are simulated.
256 devices in a mesh: tm: 64 (over x, z, y_hi), head: 4 (over y_lo, core).
Axes of the slice: x: 4, y: 4 (y_hi: 2, y_lo: 2; y = y_hi * 2 + y_lo), z: 8, core: 2. Of those that a mesh axis runs over, the one named last changes fastest.
Arguments:
- latents: bfloat16 [49152, 3072], P('tm', 'head'), may hold values from -6 to 6
- w_query: bfloat16 [3072, 1536], P(None, 'head'), may hold values from -0.109375 to 0.109375
- w_key: bfloat16 [3072, 1536], P(None, 'head'), may hold values from -0.109375 to 0.109375
- w_value: bfloat16 [3072, 1536], P(None, 'head'), may hold values from -0.109375 to 0.109375
- q_gain: float32 [128], replicated, may hold values from 1 to 2
- k_gain: float32 [128], replicated, may hold values from 1 to 2
- w_out: bfloat16 [1536, 3072], P('head'), may hold values from -0.15625 to 0.15625
- neighbours: int32 [128, 4], P('tm'), may hold values from 0 to 127, as said below
- tile_slot: int32 [128], replicated, may hold values from 0 to 127, as said below
- slab_dest: int32 [64], replicated, may hold values from 0 to 63, as said below
Outputs:
- handed: bfloat16 [49152, 3072], P('tm', 'head')
Inputs may be any that keep to these rules, and one draw needn't show every extreme that they name: `neighbours`: entry 0 of row g is g; the other 3 entries of a row are distinct tiles other than g from the slabs g // 2 - 1, g // 2 and g // 2 + 1 that exist. A permutation that keeps every tile in its own slab: tile_slot[g] // 2 == g // 2. slab_dest[s] = (s + r) % 64 for one r of 1 to 63.
All inputs are finite; a program needn't handle non-finite values.
Results may differ from a plain program's by a relative error of at most 0.012.
Values may be sent and summed in bfloat16 or wider, within the bound.
A program may use at most 128 MiB of HBM per device.

v0:
```python
import functools
import math

import jax
import jax.numpy as jnp
from jax import lax
from jax.experimental import pallas as pl
from jax.experimental.pallas import tpu as pltpu
from jax.sharding import PartitionSpec as P

HEAD_DIM = 128
MESH = pl.DeviceIdType.MESH
STEPS = 4
VMEM_LIMIT = 56 * 2**20


def other(tm):
    return tm + 1 - 2 * (tm % 2)


def core_mate(head):
    return head + 1 - 2 * (head % 2)


def across(head):
    return (head + 2) % 4


def normed(values_in, gain):
    mean_square = jnp.mean(values_in * values_in, axis=-1, keepdims=True)
    return values_in * lax.rsqrt(mean_square + 1e-06) * gain


def attend_kernel(
    lat, w_query, w_key, w_value, q_gain, k_gain, w_out, nbr, slot,
    o_ref, wo_ref,
    x, w, kv, q, send, recv, wsend, wrecv, local,
):
    tm, head = lax.axis_index("tm"), lax.axis_index("head")
    n_tm = lax.axis_size("tm")
    rows, width = lat.shape
    cols = w_query.shape[1]
    heads = cols // HEAD_DIM
    step_rows = rows // STEPS
    half = step_rows // 2
    tile = rows // 2
    pair = other(tm)
    mate, far, far_mate = core_mate(head), across(head), across(core_mate(head))
    y_hi = tm % 2
    z_to = (tm + 2 - 4 * y_hi + n_tm) % n_tm
    z_from = (tm - 2 + 4 * y_hi + n_tm) % n_tm

    loads = [
        pltpu.make_async_copy(lat, x.at[0, :, pl.ds(pl.multiple_of(head * width, width), width)], local.at[0]),
        pltpu.make_async_copy(w_query, w.at[:, pl.ds(0, cols)], local.at[1]),
        pltpu.make_async_copy(w_key, w.at[:, pl.ds(cols, cols)], local.at[2]),
        pltpu.make_async_copy(w_value, w.at[:, pl.ds(2 * cols, cols)], local.at[3]),
        pltpu.make_async_copy(
            w_out.at[:, pl.ds(pl.multiple_of(head * width, width), width)],
            wo_ref.at[pl.ds(pl.multiple_of(head * cols, cols), cols), :], local.at[4]),
    ]
    for copy in loads:
        copy.start()

    barrier = pltpu.get_barrier_semaphore()
    for device in ((tm, mate), (tm, far), (pair, far), (pair, far_mate), (z_from, head)):
        pl.semaphore_signal(barrier, inc=1, device_id=device, device_id_type=MESH)
    pl.semaphore_wait(barrier, 5)

    def band(slab, start, count, owner):
        return x.at[slab, pl.ds(start, count), pl.ds(pl.multiple_of(owner * width, width), width)]

    def copy(src, dst, kind, step, device):
        return pltpu.make_async_remote_copy(
            src_ref=src, dst_ref=dst, send_sem=send.at[kind, step], recv_sem=recv.at[kind, step],
            device_id=device, device_id_type=MESH)

    def at(step):
        return pl.multiple_of(step * step_rows, step_rows)

    def own_far(p):
        return copy(lat.at[pl.ds(at(p), step_rows), :], band(0, at(p), step_rows, head), 0, p, (tm, far))

    def own_pair(p):
        return copy(lat.at[pl.ds(at(p), step_rows), :], band(1, at(p), step_rows, head), 1, p, (pair, far))

    def relay_far(p):
        src = band(0, at(p), half, far)
        return copy(src, band(1, at(p), half, far), 2, p, (pair, far))

    def relay_pair(p):
        src = band(1, at(p) + half, half, far)
        return copy(src, band(1, at(p) + half, half, far), 3, p, (tm, far))

    def mate_own():
        return copy(lat, band(0, 0, rows, head), 4, 0, (tm, mate))

    def mate_far(p):
        block = band(0, at(p), step_rows, far)
        return copy(block, block, 5, p, (tm, mate))

    def mate_pair(p):
        block = band(1, at(p), step_rows, far)
        return copy(block, block, 6, p, (tm, mate))

    def mate_relayed(p):
        block = band(1, at(p), step_rows, head)
        return copy(block, block, 7, p, (tm, mate))

    def arrived(dst, kind, step):
        copy(dst, dst, kind, step, (tm, mate)).wait_recv()

    def kv_rows(slab, p):
        return kv.at[2 * slab + p // 2, pl.ds(pl.multiple_of((p % 2) * step_rows, step_rows), step_rows), :]

    def z_copy(p):
        return copy(kv_rows(1, p), kv_rows(2, p), 8, p, (z_to, head))

    def wo_part(owner):
        return w_out.at[:, pl.ds(pl.multiple_of(owner * width, width), width)]

    def wo_rows(owner):
        return wo_ref.at[pl.ds(pl.multiple_of(owner * cols, cols), cols), :]

    def wo_copy(k, owner, device):
        return pltpu.make_async_remote_copy(
            src_ref=wo_part(owner), dst_ref=wo_rows(head), send_sem=wsend.at[k], recv_sem=wrecv.at[k],
            device_id=device, device_id_type=MESH)

    wo_copies = [
        wo_copy(0, mate, (tm, mate)),
        wo_copy(1, far, (tm, far)),
        wo_copy(2, far_mate, (pair, far_mate)),
    ]

    for p in range(2):
        own_far(p).start()
        own_pair(p).start()
    mate_own().start()
    for copy_in in loads:
        copy_in.wait()
    arrived(band(0, 0, rows, mate), 4, 0)

    def store_kv(slab, m, key_sums, value_sums):
        b, r = 2 * slab + m // 2, pl.ds(pl.multiple_of((m % 2) * step_rows, step_rows), step_rows)
        for h in range(heads):
            c = slice(h * HEAD_DIM, (h + 1) * HEAD_DIM)
            kv[b, r, c] = normed(key_sums[:, c], k_gain[...]).astype(jnp.bfloat16)
        kv[b, r, cols:] = value_sums.astype(jnp.bfloat16)

    def step(p, carry):
        @pl.when(p < STEPS)
        def _():
            arrived(band(0, at(p), step_rows, far), 0, p)
            relay_far(p).start()
            mate_far(p).start()
            arrived(band(1, at(p), step_rows, far), 1, p)
            relay_pair(p).start()
            mate_pair(p).start()

        @pl.when(p < STEPS - 2)
        def _():
            own_far(p + 2).start()
            own_pair(p + 2).start()

        @pl.when(p == STEPS)
        def _():
            for c in wo_copies:
                c.start()

        @pl.when(p >= 1)
        def _():
            m = p - 1
            arrived(band(1, at(m), half, head), 2, m)
            arrived(band(1, at(m) + half, half, head), 3, m)
            mate_relayed(m).start()
            arrived(band(0, at(m), step_rows, far_mate), 5, m)
            arrived(band(1, at(m), step_rows, far_mate), 6, m)
            arrived(band(1, at(m), step_rows, mate), 7, m)
            sums = jnp.dot(x[1, pl.ds(at(m), step_rows), :], w[:, cols:], preferred_element_type=jnp.float32)
            store_kv(1, m, sums[:, :cols], sums[:, cols:])
            z_copy(m).start()
            sums = jnp.dot(x[0, pl.ds(at(m), step_rows), :], w[...], preferred_element_type=jnp.float32)
            for h in range(heads):
                c = slice(h * HEAD_DIM, (h + 1) * HEAD_DIM)
                q[pl.ds(at(m), step_rows), c] = normed(sums[:, c], q_gain[...]).astype(jnp.bfloat16)
            store_kv(0, m, sums[:, cols:2 * cols], sums[:, 2 * cols:])

        return carry

    lax.fori_loop(0, STEPS + 1, step, 0)

    def drain(p, carry):
        for c in (own_far(p), own_pair(p), relay_far(p), relay_pair(p), mate_far(p), mate_pair(p), mate_relayed(p)):
            c.wait_send()
        arrived(kv_rows(2, p), 8, p)
        z_copy(p).wait_send()
        return carry

    lax.fori_loop(0, STEPS, drain, 0)
    mate_own().wait_send()

    scaling = 1.0 / math.sqrt(HEAD_DIM)
    base = 2 * tm
    first = slot[base] - base

    def attend(b, carry):
        t = jnp.clip(first + b - 2 * first * b, 0, 1)
        places = []
        for j in range(nbr.shape[1]):
            block = slot[jnp.clip(nbr[t, j], 0, slot.shape[0] - 1)] - base
            block = jnp.where(block < 0, block + 6 - 2 * y_hi, jnp.where(block >= 2, block + 2 * y_hi, block))
            places.append(jnp.clip(block, 0, kv.shape[0] - 1))
        r = pl.ds(pl.multiple_of(b * tile, tile), tile)
        for h in range(heads):
            c = slice(h * HEAD_DIM, (h + 1) * HEAD_DIM)
            cv = slice(cols + h * HEAD_DIM, cols + (h + 1) * HEAD_DIM)
            qh = q[r, c]
            total, out = None, None
            for place in places:
                scores = lax.dot_general(
                    qh, kv[place, :, c], (((1,), (1,)), ((), ())), preferred_element_type=jnp.float32)
                raised = jnp.exp(scores * scaling)
                part = jnp.sum(raised, axis=-1, keepdims=True)
                got = jnp.dot(raised.astype(jnp.bfloat16), kv[place, :, cv], preferred_element_type=jnp.float32)
                total = part if total is None else total + part
                out = got if out is None else out + got
            o_ref[r, c] = (out / total).astype(jnp.bfloat16)
        return carry

    lax.fori_loop(0, 2, attend, 0)

    for k, owner in enumerate((mate, far, far_mate)):
        wo_copies[k].wait_send()
        pltpu.make_async_remote_copy(
            src_ref=wo_rows(owner), dst_ref=wo_rows(owner), send_sem=wsend.at[k], recv_sem=wrecv.at[k],
            device_id=(tm, mate), device_id_type=MESH).wait_recv()


def hand_kernel(r, o, g, send, recv):
    tm, head = lax.axis_index("tm"), lax.axis_index("head")
    n_tm = lax.axis_size("tm")
    rows, cols = o.shape
    mate, far, far_mate = core_mate(head), across(head), across(core_mate(head))
    to, source = (tm + r) % n_tm, (tm - r + n_tm) % n_tm
    step_rows = rows // STEPS

    def band(start, count, owner):
        return g.at[pl.ds(start, count), pl.ds(pl.multiple_of(owner * cols, cols), cols)]

    def at(step):
        return pl.multiple_of(step * step_rows, step_rows)

    barrier = pltpu.get_barrier_semaphore()
    for device in ((tm, mate), (tm, far), (source, head)):
        pl.semaphore_signal(barrier, inc=1, device_id=device, device_id_type=MESH)
    pl.semaphore_wait(barrier, 3)

    def copy(src, dst, kind, step, device):
        return pltpu.make_async_remote_copy(
            src_ref=src, dst_ref=dst, send_sem=send.at[kind, step], recv_sem=recv.at[kind, step],
            device_id=device, device_id_type=MESH)

    def hand(p):
        return copy(o.at[pl.ds(at(p), step_rows), :], band(at(p), step_rows, head), 0, p, (to, head))

    def pass_on(p, owner, kind, device):
        block = band(at(p), step_rows, owner)
        return copy(block, block, kind, p, device)

    def start(p, carry):
        hand(p).start()
        return carry

    def first(p, carry):
        pass_on(p, head, 0, (tm, mate)).wait_recv()
        pass_on(p, head, 1, (tm, far)).start()
        pass_on(p, head, 2, (tm, mate)).start()
        return carry

    def second(p, carry):
        pass_on(p, far, 1, (tm, mate)).wait_recv()
        pass_on(p, far, 3, (tm, mate)).start()
        return carry

    def last(p, carry):
        pass_on(p, mate, 2, (tm, mate)).wait_recv()
        pass_on(p, far_mate, 3, (tm, mate)).wait_recv()
        hand(p).wait_send()
        pass_on(p, head, 1, (tm, far)).wait_send()
        pass_on(p, head, 2, (tm, mate)).wait_send()
        pass_on(p, far, 3, (tm, mate)).wait_send()
        return carry

    for body in (start, first, second, last):
        lax.fori_loop(0, STEPS, body, 0)


def handed_over(r, o):
    rows, cols = o.shape
    return pl.pallas_call(
        functools.partial(hand_kernel, r),
        name="hand",
        out_shape=jax.ShapeDtypeStruct((rows, 4 * cols), jnp.bfloat16),
        in_specs=[pl.BlockSpec(memory_space=pl.ANY)],
        out_specs=pl.BlockSpec(memory_space=pl.ANY),
        scratch_shapes=[
            pltpu.SemaphoreType.DMA((4, STEPS)),
            pltpu.SemaphoreType.DMA((4, STEPS)),
        ],
        compiler_params=pltpu.CompilerParams(
            collective_id=2 + r, has_side_effects=True, vmem_limit_bytes=VMEM_LIMIT
        ),
    )(o)


def product_kernel(g, wo, out):
    step_rows = 256
    def step(p, carry):
        r = pl.ds(pl.multiple_of(p * step_rows, step_rows), step_rows)
        out[r, :] = jnp.dot(g[r, :], wo[...], preferred_element_type=jnp.float32).astype(jnp.bfloat16)
        return carry
    lax.fori_loop(0, out.shape[0] // step_rows, step, 0)


def per_device(
    latents, w_query, w_key, w_value, q_gain, k_gain, w_out, neighbours, tile_slot, slab_dest
):
    rows, width = latents.shape
    cols = w_query.shape[1]
    any_spec = pl.BlockSpec(memory_space=pl.ANY)
    vmem_spec = pl.BlockSpec(memory_space=pltpu.VMEM)
    smem_spec = pl.BlockSpec(memory_space=pltpu.SMEM)
    bf16 = jnp.bfloat16
    attention, wo = pl.pallas_call(
        attend_kernel,
        name="attend",
        out_shape=(
            jax.ShapeDtypeStruct((rows, cols), bf16),
            jax.ShapeDtypeStruct((4 * cols, width), bf16),
        ),
        in_specs=[any_spec] * 4 + [vmem_spec] * 2 + [any_spec] + [smem_spec] * 2,
        out_specs=(vmem_spec, vmem_spec),
        scratch_shapes=[
            pltpu.VMEM((2, rows, 4 * width), bf16),
            pltpu.VMEM((4 * width, 3 * cols), bf16),
            pltpu.VMEM((6, rows // 2, 2 * cols), bf16),
            pltpu.VMEM((rows, cols), bf16),
            pltpu.SemaphoreType.DMA((9, STEPS)),
            pltpu.SemaphoreType.DMA((9, STEPS)),
            pltpu.SemaphoreType.DMA((3,)),
            pltpu.SemaphoreType.DMA((3,)),
            pltpu.SemaphoreType.DMA((5,)),
        ],
        compiler_params=pltpu.CompilerParams(
            collective_id=1, has_side_effects=True, vmem_limit_bytes=VMEM_LIMIT
        ),
    )(
        latents, w_query, w_key, w_value, q_gain.reshape(1, -1), k_gain.reshape(1, -1), w_out, neighbours, tile_slot
    )
    n_tm = lax.axis_size("tm")
    hands = [functools.partial(handed_over, r) for r in range(1, n_tm)]
    gathered = lax.switch(slab_dest[0] - 1, hands, attention)
    return pl.pallas_call(
        product_kernel,
        name="product",
        out_shape=jax.ShapeDtypeStruct((rows, width), bf16),
        in_specs=[vmem_spec, vmem_spec],
        out_specs=vmem_spec,
        compiler_params=pltpu.CompilerParams(vmem_limit_bytes=VMEM_LIMIT),
    )(gathered, wo)


def solution(mesh):
    return jax.shard_map(
        per_device,
        mesh=mesh,
        in_specs=(
            P("tm", "head"),
            P(None, "head"),
            P(None, "head"),
            P(None, "head"),
            P(),
            P(),
            P("head", None),
            P("tm", None),
            P(),
            P(),
        ),
        out_specs=P("tm", "head"),
        check_vma=False,
    )
```

profile of v0, /device:TPU:1, one launch (start us, length us, event | category | flops | bytes accessed | tf_op | source)
XLA Modules:
  0.0 103.4 jit_solution(9181028973587730203)
XLA Ops:
  0.7 72.6 %attend.1 = (bf16[768,384]{1,0:T(8,128)(2,1)S(1)}, bf16[1536,768]{1,0:T(8,128)(2,1)}) custom-call(bf16[768,768]{1,0:T(8,128)(2,1)} %lat.1, bf16[3072,384]{1,0:T(8,128)(2,1)} %w_query.1, bf16[3072,384]{1,0:T(8,128)(2,1)} %w_key.1, bf16[3072,384]{1,0:T(8,128)(2,1)} %w_value.1, f32[1,128]{1,0:T(1,128)} %bitcast.4, f32[1,128]{1,0:T(1,128)} %bitcast.5, ...), custom_call_target="tpu_custom_call" | custom-call | tf_op jit(solution)/shard_map/attend/pallas_call | solution.py:335
  73.3 25.1 %conditional.1 = (bf16[768,1536]{1,0:T(8,128)(2,1)S(1)}) conditional(s32[]{:T(128)} %bitcast, bf16[768,384]{1,0:T(8,128)(2,1)S(1)} %get-tuple-element.134, bf16[768,384]{1,0:T(8,128)(2,1)S(1)} %get-tuple-element.134, bf16[768,384]{1,0:T(8,128)(2,1)S(1)} %get-tuple-element.134, ...), branch_computations={%region_0.0_spmd, %region_1.0_spmd, %region_2.0_spmd, %region_3.0_... | conditional | bytes 8 | solution.py:363
  73.3 24.6 %hand.78 = bf16[768,1536]{1,0:T(8,128)(2,1)S(1)} custom-call(bf16[768,384]{1,0:T(8,128)(2,1)S(1)} %o.15), custom_call_target="tpu_custom_call" | custom-call | tf_op jit(solution)/shard_map/cond/branch_15_fun/hand/pallas_call | solution.py:301
  98.4 5.0 %product.1 = bf16[768,768]{1,0:T(8,128)(2,1)} custom-call(bf16[768,1536]{1,0:T(8,128)(2,1)S(1)} %get-tuple-element.136.g, bf16[1536,768]{1,0:T(8,128)(2,1)} %get-tuple-element.135.wo), custom_call_target="tpu_custom_call" | custom-call | tf_op jit(solution)/shard_map/product/pallas_call | solution.py:364
where the time goes:
time: 104 us; the launch traced here: 103 us
  Pallas kernels  102 us (98%)
    pallas_call x1, Pallas kernels, per_device(): pl.pallas_call(attend_kernel, name='attend', out_shape=(jax.ShapeDtypeStr...  72.6 us
    pallas_call x1, Pallas kernels, handed_over(): pl.pallas_call(functools.partial(hand_kernel, r), name='hand', out_shape=...  24.6 us
    pallas_call x1, Pallas kernels, per_device(): pl.pallas_call(product_kernel, name='product', out_shape=jax.ShapeDtypeSt...  5.01 us

commit v1 on v0

--- a/solution.py
+++ b/solution.py
@@ -11,6 +11,11 @@
 HEAD_DIM = 128
 MESH = pl.DeviceIdType.MESH
 STEPS = 4
+SAME_X = 16
+N_Z = 8
+CHUNKS = 8
+HAND_LIMIT = 4 * 2**20
+PRODUCT_LIMIT = 16 * 2**20
 VMEM_LIMIT = 56 * 2**20
 
 
@@ -59,9 +64,6 @@
             w_out.at[:, pl.ds(pl.multiple_of(head * width, width), width)],
             wo_ref.at[pl.ds(pl.multiple_of(head * cols, cols), cols), :], local.at[4]),
     ]
-    for copy in loads:
-        copy.start()
-
     barrier = pltpu.get_barrier_semaphore()
     for device in ((tm, mate), (tm, far), (pair, far), (pair, far_mate), (z_from, head)):
         pl.semaphore_signal(barrier, inc=1, device_id=device, device_id_type=MESH)
@@ -136,9 +138,11 @@
     for p in range(2):
         own_far(p).start()
         own_pair(p).start()
+    for load in loads:
+        load.start()
     mate_own().start()
-    for copy_in in loads:
-        copy_in.wait()
+    for load in loads:
+        load.wait()
     arrived(band(0, 0, rows, mate), 4, 0)
 
     def store_kv(slab, m, key_sums, value_sums):
@@ -237,63 +241,124 @@
             device_id=(tm, mate), device_id_type=MESH).wait_recv()
 
 
-def hand_kernel(r, o, g, send, recv):
+def z_moved(tm, by):
+    return tm // SAME_X * SAME_X + (tm // 2 % N_Z + by + N_Z) % N_Z * 2 + tm % 2
+
+
+def way_round(distance):
+    if distance in (2, N_Z - 2):
+        return 2, -3 if distance == 2 else 3
+    if distance in (3, N_Z - 3):
+        return 3, -2 if distance == 3 else 2
+    return 0, 0
+
+
+def hand_kernel(r, o, g, relayed, recv, sent, joined, passed):
     tm, head = lax.axis_index("tm"), lax.axis_index("head")
     n_tm = lax.axis_size("tm")
     rows, cols = o.shape
+    chunk_rows = rows // CHUNKS
     mate, far, far_mate = core_mate(head), across(head), across(core_mate(head))
     to, source = (tm + r) % n_tm, (tm - r + n_tm) % n_tm
-    step_rows = rows // STEPS
+    (n_low, by_low), (n_high, by_high) = way_round(r // 2 % N_Z), way_round((r + 1) // 2 % N_Z)
+    relays = n_low + n_high > 0
+
+    def either(low, high, device):
+        return low if low == high else low + (high - low) * (device % 2)
+
+    n_mine, n_source = either(n_low, n_high, tm), either(n_low, n_high, source)
+    relay = z_moved(tm, either(by_low, by_high, tm))
+    relay_for = z_moved(tm, -either(by_low, by_high, tm))
+    relay_to = (relay_for + r) % n_tm
+    source_relay = z_moved(source, either(by_low, by_high, source))
+
+    def when(count, act):
+        if isinstance(count, int):
+            if count:
+                act()
+        else:
+            pl.when(count > 0)(act)
 
     def band(start, count, owner):
         return g.at[pl.ds(start, count), pl.ds(pl.multiple_of(owner * cols, cols), cols)]
 
-    def at(step):
-        return pl.multiple_of(step * step_rows, step_rows)
+    def at(p):
+        return pl.multiple_of(p * chunk_rows, chunk_rows)
+
+    def own(p):
+        return o.at[pl.ds(at(p), chunk_rows), :]
 
     barrier = pltpu.get_barrier_semaphore()
+
+    def greet(device):
+        pl.semaphore_signal(barrier, inc=1, device_id=device, device_id_type=MESH)
+
     for device in ((tm, mate), (tm, far), (source, head)):
-        pl.semaphore_signal(barrier, inc=1, device_id=device, device_id_type=MESH)
-    pl.semaphore_wait(barrier, 3)
-
-    def copy(src, dst, kind, step, device):
+        greet(device)
+    if relays:
+        when(n_mine, lambda: greet((relay_for, head)))
+        when(n_source, lambda: greet((source_relay, head)))
+    pl.semaphore_wait(barrier, either(5 if n_low else 3, 5 if n_high else 3, tm))
+
+    def copy(src, dst, device, arrival, departure=None):
         return pltpu.make_async_remote_copy(
-            src_ref=src, dst_ref=dst, send_sem=send.at[kind, step], recv_sem=recv.at[kind, step],
+            src_ref=src, dst_ref=dst, send_sem=sent if departure is None else departure, recv_sem=arrival,
             device_id=device, device_id_type=MESH)
 
     def hand(p):
-        return copy(o.at[pl.ds(at(p), step_rows), :], band(at(p), step_rows, head), 0, p, (to, head))
-
-    def pass_on(p, owner, kind, device):
-        block = band(at(p), step_rows, owner)
-        return copy(block, block, kind, p, device)
-
-    def start(p, carry):
-        hand(p).start()
-        return carry
-
-    def first(p, carry):
-        pass_on(p, head, 0, (tm, mate)).wait_recv()
-        pass_on(p, head, 1, (tm, far)).start()
-        pass_on(p, head, 2, (tm, mate)).start()
-        return carry
-
-    def second(p, carry):
-        pass_on(p, far, 1, (tm, mate)).wait_recv()
-        pass_on(p, far, 3, (tm, mate)).start()
-        return carry
-
-    def last(p, carry):
-        pass_on(p, mate, 2, (tm, mate)).wait_recv()
-        pass_on(p, far_mate, 3, (tm, mate)).wait_recv()
-        hand(p).wait_send()
-        pass_on(p, head, 1, (tm, far)).wait_send()
-        pass_on(p, head, 2, (tm, mate)).wait_send()
-        pass_on(p, far, 3, (tm, mate)).wait_send()
-        return carry
-
-    for body in (start, first, second, last):
-        lax.fori_loop(0, STEPS, body, 0)
+        return copy(own(p), band(at(p), chunk_rows, head), (to, head), recv.at[0, p])
+
+    def to_relay(p):
+        return copy(own(p), relayed.at[p], (relay, head), recv.at[2, p])
+
+    def from_relay(p):
+        return copy(relayed.at[p], band(at(p), chunk_rows, head), (relay_to, head), recv.at[0, p], passed.at[p])
+
+    def pass_on(p, owner, device, arrival):
+        block = band(at(p), chunk_rows, owner)
+        return copy(block, block, device, arrival)
+
+    def loop(low, high, act):
+        def body(p, carry):
+            act(p)
+            return carry
+        lax.fori_loop(low, high, body, 0)
+
+    if relays:
+        loop(0, n_mine, lambda p: to_relay(p).start())
+    loop(n_mine, CHUNKS, lambda p: hand(p).start())
+
+    def relay_one(p):
+        to_relay(p).wait_recv()
+        from_relay(p).start()
+
+    if relays:
+        loop(0, n_mine, relay_one)
+
+    def spread(k):
+        p = k
+        if relays:
+            turned = jnp.logical_and(k % 2 == 1, k // 2 < n_source)
+            p = jnp.where(turned, k // 2, n_source + k - jnp.minimum((k + 1) // 2, n_source))
+        pass_on(p, head, (tm, mate), recv.at[0, p]).wait_recv()
+        pass_on(p, head, (tm, far), recv.at[1, p]).start()
+        pass_on(p, head, (tm, mate), joined).start()
+
+    def second(k):
+        p = k
+        if relays:
+            turned = jnp.logical_and(k % 2 == 1, k // 2 < n_source)
+            p = jnp.where(turned, k // 2, n_source + k - jnp.minimum((k + 1) // 2, n_source))
+        pass_on(p, far, (tm, mate), recv.at[1, p]).wait_recv()
+        pass_on(p, far, (tm, mate), joined).start()
+
+    loop(0, CHUNKS, spread)
+    loop(0, CHUNKS, second)
+    two = g.at[:, pl.ds(0, 2 * cols)]
+    copy(two, two, (tm, mate), joined).wait_recv()
+    copy(g, g, (tm, mate), joined).wait_send()
+    if relays:
+        loop(0, n_mine, lambda p: from_relay(p).wait_send())
 
 
 def handed_over(r, o):
@@ -305,22 +370,20 @@
         in_specs=[pl.BlockSpec(memory_space=pl.ANY)],
         out_specs=pl.BlockSpec(memory_space=pl.ANY),
         scratch_shapes=[
-            pltpu.SemaphoreType.DMA((4, STEPS)),
-            pltpu.SemaphoreType.DMA((4, STEPS)),
+            pltpu.VMEM((3, rows // CHUNKS, cols), jnp.bfloat16),
+            pltpu.SemaphoreType.DMA((3, CHUNKS)),
+            pltpu.SemaphoreType.DMA,
+            pltpu.SemaphoreType.DMA,
+            pltpu.SemaphoreType.DMA((3,)),
         ],
         compiler_params=pltpu.CompilerParams(
-            collective_id=2 + r, has_side_effects=True, vmem_limit_bytes=VMEM_LIMIT
+            collective_id=2 + r, has_side_effects=True, vmem_limit_bytes=HAND_LIMIT
         ),
     )(o)
 
 
 def product_kernel(g, wo, out):
-    step_rows = 256
-    def step(p, carry):
-        r = pl.ds(pl.multiple_of(p * step_rows, step_rows), step_rows)
-        out[r, :] = jnp.dot(g[r, :], wo[...], preferred_element_type=jnp.float32).astype(jnp.bfloat16)
-        return carry
-    lax.fori_loop(0, out.shape[0] // step_rows, step, 0)
+    out[...] = jnp.dot(g[...], wo[...], preferred_element_type=jnp.float32).astype(jnp.bfloat16)
 
 
 def per_device(
@@ -365,9 +428,13 @@
         product_kernel,
         name="product",
         out_shape=jax.ShapeDtypeStruct((rows, width), bf16),
-        in_specs=[vmem_spec, vmem_spec],
-        out_specs=vmem_spec,
-        compiler_params=pltpu.CompilerParams(vmem_limit_bytes=VMEM_LIMIT),
+        grid=(3,),
+        in_specs=[
+            pl.BlockSpec((rows // 3, 4 * cols), lambda i: (i, 0)),
+            pl.BlockSpec((4 * cols, width), lambda i: (0, 0)),
+        ],
+        out_specs=pl.BlockSpec((rows // 3, width), lambda i: (i, 0)),
+        compiler_params=pltpu.CompilerParams(vmem_limit_bytes=PRODUCT_LIMIT),
     )(gathered, wo)
 
 

time: 104 us -> 120 us (1.15)
  Pallas kernels: 102 us -> 119 us
    pallas_call x1, Pallas kernels: 24.6 us -> 41.4 us  [handed_over(): pl.pallas_call(functools.partial(hand_kernel, r), name='hand', out_shape=...]
where the time goes in v1:
time: 120 us
  Pallas kernels  119 us (99%)
    pallas_call x1, Pallas kernels, per_device(): pl.pallas_call(attend_kernel, name='attend', out_shape=(jax.ShapeDtypeStr...  72.6 us
    pallas_call x1, Pallas kernels, handed_over(): pl.pallas_call(functools.partial(hand_kernel, r), name='hand', out_shape=...  41.4 us
    pallas_call x1, Pallas kernels, per_device(): pl.pallas_call(product_kernel, name='product', out_shape=jax.ShapeDtypeSt...  4.73 us

profile of v1, /device:TPU:1, one launch (start us, length us, event | category | flops | bytes accessed | tf_op | source)
XLA Modules:
  0.0 120.0 jit_solution(3449288212047925124)
XLA Ops:
  0.7 72.6 %attend.1 = (bf16[768,384]{1,0:T(8,128)(2,1)S(1)}, bf16[1536,768]{1,0:T(8,128)(2,1)}) custom-call(bf16[768,768]{1,0:T(8,128)(2,1)} %lat.1, bf16[3072,384]{1,0:T(8,128)(2,1)} %w_query.1, bf16[3072,384]{1,0:T(8,128)(2,1)} %w_key.1, bf16[3072,384]{1,0:T(8,128)(2,1)} %w_value.1, f32[1,128]{1,0:T(1,128)} %bitcast.4, f32[1,128]{1,0:T(1,128)} %bitcast.5, ...), custom_call_target="tpu_custom_call" | custom-call | tf_op jit(solution)/shard_map/attend/pallas_call | solution.py:398
  73.3 0.0 copy-start
  73.3 41.9 %conditional.1 = (bf16[768,1536]{1,0:T(8,128)(2,1)}) conditional(s32[]{:T(128)} %bitcast, bf16[768,384]{1,0:T(8,128)(2,1)S(1)} %get-tuple-element.134, bf16[768,384]{1,0:T(8,128)(2,1)S(1)} %get-tuple-element.134, bf16[768,384]{1,0:T(8,128)(2,1)S(1)} %get-tuple-element.134, ...), branch_computations={%region_0.0_spmd, %region_1.0_spmd, %region_2.0_spmd, %region_3.0_... | conditional | bytes 8 | solution.py:426
  73.4 41.4 %hand.84 = bf16[768,1536]{1,0:T(8,128)(2,1)} custom-call(bf16[768,384]{1,0:T(8,128)(2,1)S(1)} %o.21), custom_call_target="tpu_custom_call" | custom-call | tf_op jit(solution)/shard_map/cond/branch_21_fun/hand/pallas_call | solution.py:366
  115.2 0.0 copy-done
  115.2 4.7 %product.1 = bf16[768,768]{1,0:T(8,128)(2,1)} custom-call(bf16[768,1536]{1,0:T(8,128)(2,1)} %get-tuple-element.136.g, bf16[1536,768]{1,0:T(8,128)(2,1)S(1)} %copy-done), custom_call_target="tpu_custom_call" | custom-call | tf_op jit(solution)/shard_map/product/pallas_call | solution.py:427
Async XLA Ops:
  73.3 41.9 %copy-start = (bf16[1536,768]{1,0:T(8,128)(2,1)S(1)}, bf16[1536,768]{1,0:T(8,128)(2,1)}, u32[]{:S(2)}) copy-start(bf16[1536,768]{1,0:T(8,128)(2,1)} %get-tuple-element.135.wo) | copy-start | bytes 7077892
